TPU v7x, 32 devices: a whole 2x2x4 slice. The times are simulated.
32 devices in a mesh: grp: 2 (over y), seq: 4 (over z), head: 4 (over x, core).
Axes of the slice: x: 2, y: 2, z: 4, core: 2. Of those that a mesh axis runs over, the one named last changes fastest.
Arguments:
- q_heads: bfloat16 [8, 64, 16384], P('head', None, ('grp', 'seq')), parts along dimension 2, may hold values from -12 to 12
- k_heads: bfloat16 [8, 64, 16384], P('head', None, ('grp', 'seq')), parts along dimension 2, may hold values from -10 to 10
- v_heads: bfloat16 [8, 64, 16384], P('head', None, ('grp', 'seq')), parts along dimension 2, may hold values from -10 to 10
- morton_order: int32 [8, 2048], P(('grp', 'seq')), parts along dimension 0, may hold values from 0 to 2047, each once within a row
- leaf_counts: int32 [64], P('grp'), parts along dimension 0, may hold values from 64 to 256, as said below
Outputs:
- attended: bfloat16 [8, 64, 16384], P('head', None, ('grp', 'seq')), parts along dimension 2
There are 2 independent parts, one for each index of `grp`. A program takes and returns all parts, laid end to end along the dimension named above; each array names one. Nothing has to cross between parts.
Inputs may be any that keep to these rules, and one draw needn't show every extreme that they name: `morton_order`: each row holds every number of 0 .. 2047 once. `leaf_counts`: the valid points of a leaf are its first ones.
All inputs are finite; a program needn't handle non-finite values.
Results may differ from a plain program's by a relative error of at most 0.0021.
Values may be sent and summed in bfloat16 or wider, within the bound.
A program may use at most 64 MiB of HBM per device.

v0:
```python
import functools
import math

import jax
import jax.numpy as jnp
from jax import lax
from jax.experimental import pallas as pl
from jax.experimental.pallas import tpu as pltpu
from jax.sharding import PartitionSpec as P

LEAF = 256
NEG = -1e30
BF = jnp.bfloat16
F32 = jnp.float32
PAD = 16


def dot(a, b, dims=((1,), (0,))):
    return lax.dot_general(a, b, (dims, ((), ())), preferred_element_type=F32)


def split(x):
    hi = x.astype(BF)
    return hi, (x - hi.astype(F32)).astype(BF)


def kernel(cfg, *refs):
    heads, width, tokens, seq_count = cfg
    rows = heads * width
    leaves = tokens // LEAF
    depth_local = leaves.bit_length() - 1
    depth_all = (leaves * seq_count).bit_length() - 1
    levels = list(range(1, depth_all))
    far_levels = [l for l in levels if l >= depth_local]
    scale = math.log2(math.e) / math.sqrt(width)
    refs = list(refs)
    take = lambda n: [refs.pop(0) for _ in range(n)]
    q_hbm, k_hbm, v_hbm, order, counts, out = take(6)
    xin, xp, kva, ktx, vx, num, stat = take(7)
    us = dict(zip(levels, take(len(levels))))
    fs = dict(zip(levels, take(len(levels))))
    qs = dict(zip(far_levels, take(len(far_levels))))
    kmp = dict(zip(far_levels, take(len(far_levels))))
    vvp = dict(zip(far_levels, take(len(far_levels))))
    kmr = dict(zip(far_levels, take(len(far_levels))))
    vvr = dict(zip(far_levels, take(len(far_levels))))
    in_sem, halo_send, halo_recv = take(3)
    far_send = dict(zip(far_levels, take(len(far_levels))))
    far_recv = dict(zip(far_levels, take(len(far_levels))))

    seq = lax.axis_index("seq")
    has_left, has_right = seq > 0, seq < seq_count - 1

    loads = [
        pltpu.make_async_copy(src, xin.at[pl.ds(i * rows, rows)], in_sem.at[i])
        for i, src in enumerate((q_hbm, k_hbm, v_hbm))
    ]
    for load in loads:
        load.start()
    barrier = pltpu.get_barrier_semaphore()
    for step in range(1, seq_count):
        other = lax.rem(seq + step, seq_count)
        pl.semaphore_signal(
            barrier, inc=1, device_id={"seq": other}, device_id_type=pl.DeviceIdType.MESH
        )

    @pl.when(jnp.logical_not(has_left))
    def _():
        ktx[0:LEAF, :] = jnp.zeros((LEAF, rows), BF)
        vx[:, 0:LEAF] = jnp.zeros((rows, LEAF), BF)

    @pl.when(jnp.logical_not(has_right))
    def _():
        ktx[tokens + LEAF :, :] = jnp.zeros((LEAF, rows), BF)
        vx[:, tokens + LEAF :] = jnp.zeros((rows, LEAF), BF)

    def count_of(n):
        leaf = seq * leaves + n
        total = leaves * seq_count
        inside = jnp.logical_and(leaf >= 0, leaf < total)
        return jnp.where(inside, counts[jnp.clip(leaf, 0, total - 1)], 0)

    def build(level):
        u = us[level]
        r = lax.broadcasted_iota(jnp.int32, u.shape, 0)
        t = lax.broadcasted_iota(jnp.int32, u.shape, 1)
        u[...] = jnp.where((t >> level) == r, 1.0, 0.0).astype(BF)

    for level in levels:
        build(level)
    for load in loads:
        load.wait()

    def permute(n):
        at = n * LEAF
        if not isinstance(n, int):
            at = pl.multiple_of(at, LEAF)
        picks = order[0:1, pl.ds(at, LEAF)]
        spots = lax.broadcasted_iota(jnp.int32, (tokens, LEAF), 0)
        hot = jnp.where(spots == picks, 1.0, 0.0).astype(BF)
        moved = dot(xin[...], hot)
        count = count_of(n)
        query, key, value = moved[:rows], moved[rows : 2 * rows], moved[2 * rows :]
        key_t = key.T
        on_row = lax.broadcasted_iota(jnp.int32, (rows, LEAF), 1) < count
        on_col = lax.broadcasted_iota(jnp.int32, (LEAF, rows), 0) < count
        xp[0:rows, pl.ds(at, LEAF)] = query.astype(BF)
        xp[rows : 2 * rows, pl.ds(at, LEAF)] = jnp.where(on_row, value, 0.0).astype(BF)
        xp[2 * rows :, pl.ds(at, LEAF)] = jnp.where(on_row[:PAD], 1.0, 0.0).astype(BF)
        kva[pl.ds(at, LEAF), 0:rows] = jnp.where(on_col, key_t, 0.0).astype(BF)
        kva[pl.ds(at, LEAF), rows:] = jnp.where(on_col, 1.0, 0.0).astype(BF)
        ktx[pl.ds(at + LEAF, LEAF), :] = key_t.astype(BF)
        vx[:, pl.ds(at + LEAF, LEAF)] = value.astype(BF)

    permute(0)
    permute(leaves - 1)
    pl.semaphore_wait(barrier, seq_count - 1)

    def remote(src, dst, send, recv, target):
        return pltpu.make_async_remote_copy(
            src_ref=src,
            dst_ref=dst,
            send_sem=send,
            recv_sem=recv,
            device_id={"seq": target},
            device_id_type=pl.DeviceIdType.MESH,
        )

    def halo(side):
        start, end = (LEAF, tokens + LEAF) if side == 0 else (tokens, 0)
        target = jnp.maximum(seq - 1, 0) if side == 0 else jnp.minimum(seq + 1, seq_count - 1)
        return (
            remote(
                ktx.at[pl.ds(start, LEAF)],
                ktx.at[pl.ds(end, LEAF)],
                halo_send.at[2 * side],
                halo_recv.at[2 * side],
                target,
            ),
            remote(
                vx.at[:, pl.ds(start, LEAF)],
                vx.at[:, pl.ds(end, LEAF)],
                halo_send.at[2 * side + 1],
                halo_recv.at[2 * side + 1],
                target,
            ),
        )

    @pl.when(has_left)
    def _():
        for copy in halo(0):
            copy.start()

    @pl.when(has_right)
    def _():
        for copy in halo(1):
            copy.start()

    if leaves > 2:

        @pl.loop(1, leaves - 1)
        def _(n):
            permute(n)

    def pool(level, off, span):
        u = us[level][...]
        kk = dot(u, kva[pl.ds(off, span), :])
        mass = kk[:, rows:]
        km_hi, km_lo = split(kk[:, :rows] / jnp.maximum(mass, 1.0))
        xx = dot(xp[:, pl.ds(off, span)], u, ((1,), (1,)))
        q_hi, q_lo = split(xx[:rows] * (1.0 / 2**level))
        v_hi, v_lo = split(xx[rows : 2 * rows])
        km = jnp.concatenate([km_hi, km_lo], axis=1)
        vv = jnp.concatenate([v_hi, v_lo, xx[2 * rows :].astype(BF)], axis=0)
        return (q_hi, q_lo), km, vv, mass

    def far(query, km, vvs, bias, store):
        q_hi, q_lo = query
        count = q_hi.shape[1]
        for h in range(heads):
            keep = lax.broadcasted_iota(jnp.int32, (rows, count), 0) // width == h
            zero = jnp.zeros((rows, count), F32)
            hi = jnp.where(keep, q_hi.astype(F32), zero).astype(BF)
            lo = jnp.where(keep, q_lo.astype(F32), zero).astype(BF)
            s = dot(km, jnp.concatenate([hi, hi], axis=0)) + dot(km[:, :rows], lo)
            if count <= 128:
                s = s + bias[:, :count]
            else:
                s = s + jnp.concatenate([bias[:, :128]] * (count // 128), axis=1)
            best = jnp.max(s, axis=0, keepdims=True).astype(BF)
            w_hi, w_lo = split(jnp.exp2((s - best.astype(F32)) * scale))
            step = 0
            acc = jnp.zeros((width + PAD, count), F32)
            for vv in vvs:
                keys = vv.shape[1]
                v_hi = vv[h * width : (h + 1) * width]
                v_lo = vv[rows + h * width : rows + (h + 1) * width]
                mass = vv[2 * rows :]
                left = jnp.concatenate([v_hi, mass], axis=0)
                acc = acc + dot(left, w_hi[step : step + keys])
                acc = acc + dot(left, w_lo[step : step + keys])
                low = dot(v_lo, w_hi[step : step + keys])
                acc = acc + jnp.concatenate([low, jnp.zeros((PAD, count), F32)], axis=0)
                step += keys
            a_hi, a_lo = split(acc)
            tops = jnp.broadcast_to(best.astype(F32), (PAD, count)).astype(BF)
            store(h, jnp.concatenate([a_hi, a_lo, tops], axis=0))

    def far_copies(level):
        bit = level - depth_local
        nb = 1 << bit
        part = tokens >> level
        slot = lax.rem(seq, nb)
        base = ((seq >> bit) ^ 1) << bit
        copies = []
        for j in range(nb):
            target = base + j
            copies.append(
                remote(
                    kmp[level],
                    kmr[level].at[pl.ds(pl.multiple_of(slot * part, part), part)],
                    far_send[level].at[2 * j],
                    far_recv[level].at[2 * slot],
                    target,
                )
            )
            copies.append(
                remote(
                    vvp[level],
                    vvr[level].at[slot],
                    far_send[level].at[2 * j + 1],
                    far_recv[level].at[2 * slot + 1],
                    target,
                )
            )
        return copies

    for level in reversed(far_levels):
        (q_hi, q_lo), km, vv, _ = pool(level, 0, tokens)
        qs[level][0:rows, :] = q_hi
        qs[level][rows:, :] = q_lo
        kmp[level][...] = km
        vvp[level][...] = vv
        for copy in far_copies(level):
            copy.start()

    for level in levels:
        if level in far_levels:
            continue
        span = LEAF << level
        for pair in range(tokens // span // 2):
            sides = [pool(level, (2 * pair + i) * span, span) for i in range(2)]
            for i in range(2):
                query = sides[i][0]
                _, km, vv, mass = sides[1 - i]
                bias = jnp.where(mass > 0, 0.0, NEG)
                first = (2 * pair + i) * LEAF

                def store(h, value):
                    fs[level][h, :, first : first + LEAF] = value

                far(query, km, [vv], bias, store)

    def near(n):
        at = n * LEAF
        if not isinstance(n, int):
            at = pl.multiple_of(at, LEAF)
        window = ktx[pl.ds(at, 3 * LEAF), :]
        query = xp[0:rows, pl.ds(at, LEAF)].astype(F32)
        spots = lax.broadcasted_iota(jnp.int32, (LEAF, LEAF), 0)
        for h in range(heads):
            keep = lax.broadcasted_iota(jnp.int32, (rows, LEAF), 0) // width == h
            s = dot(window, jnp.where(keep, query, 0.0).astype(BF))
            s = jnp.concatenate(
                [
                    jnp.where(spots < count_of(n - 1 + i), s[i * LEAF : (i + 1) * LEAF], NEG)
                    for i in range(3)
                ],
                axis=0,
            )
            best = jnp.max(s, axis=0, keepdims=True)
            w = jnp.exp2((s - best) * scale)
            total = jnp.sum(w, axis=0, keepdims=True)
            value = vx[h * width : (h + 1) * width, pl.ds(at, 3 * LEAF)]
            num[h * width : (h + 1) * width, pl.ds(at, LEAF)] = dot(value, w.astype(BF))
            stat[2 * h : 2 * h + 1, pl.ds(at, LEAF)] = best
            stat[2 * h + 1 : 2 * h + 2, pl.ds(at, LEAF)] = total

    if leaves > 2:

        @pl.loop(1, leaves - 1)
        def _(n):
            near(n)

    @pl.when(has_right)
    def _():
        for copy in halo(0):
            copy.wait_recv()

    @pl.when(has_left)
    def _():
        for copy in halo(1):
            copy.wait_recv()

    near(0)
    near(leaves - 1)

    for level in far_levels:
        nb = 1 << (level - depth_local)
        part = tokens >> level
        for i in range(nb):
            remote(
                kmp[level], kmr[level].at[pl.ds(i * part, part)],
                far_send[level].at[2 * i], far_recv[level].at[2 * i], seq,
            ).wait_recv()
            remote(
                vvp[level], vvr[level].at[i],
                far_send[level].at[2 * i + 1], far_recv[level].at[2 * i + 1], seq,
            ).wait_recv()
        query = (qs[level][0:rows, :], qs[level][rows:, :])
        vvs = [vvr[level][i] for i in range(nb)]
        ones = jnp.ones((PAD, 128), BF)
        mass = jnp.concatenate(
            [dot(vv[2 * rows :], ones, ((0,), (0,))) for vv in vvs], axis=0
        )
        bias = jnp.where(mass > 0, 0.0, NEG)

        def store(h, value):
            fs[level][h] = value

        far(query, kmr[level][...], vvs, bias, store)

    def finish(n):
        at = pl.multiple_of(n * LEAF, LEAF)
        for h in range(heads):
            near_best = stat[2 * h : 2 * h + 1, pl.ds(at, LEAF)]
            near_total = stat[2 * h + 1 : 2 * h + 2, pl.ds(at, LEAF)]
            blocks = []
            best = near_best
            size = width + PAD
            for level in levels:
                if level in far_levels:
                    f = fs[level][h]
                    u = us[level][:, pl.ds(at, LEAF)]
                else:
                    g = 1 << level
                    f = fs[level][h, :, pl.ds(pl.multiple_of((n >> level) * LEAF, LEAF), LEAF)]
                    u = us[level][:, pl.ds(pl.multiple_of((n & (g - 1)) * LEAF, LEAF), LEAF)]
                up = dot(f, u)
                top = up[2 * size : 2 * size + 1]
                blocks.append((up[:size] + up[size : 2 * size], top))
                best = jnp.maximum(best, top)
            factor = jnp.exp2((near_best - best) * scale)
            top = num[h * width : (h + 1) * width, pl.ds(at, LEAF)] * factor
            bottom = near_total * factor
            for block, level_best in blocks:
                factor = jnp.exp2((level_best - best) * scale)
                top = top + block[:width] * factor
                bottom = bottom + block[width : width + 1] * factor
            out[h * width : (h + 1) * width, pl.ds(at, LEAF)] = (top / bottom).astype(BF)

    @pl.loop(0, leaves)
    def _(n):
        finish(n)

    @pl.when(has_left)
    def _():
        for copy in halo(0):
            copy.wait_send()

    @pl.when(has_right)
    def _():
        for copy in halo(1):
            copy.wait_send()

    for level in far_levels:
        for copy in far_copies(level):
            copy.wait_send()


def shards(q_heads, k_heads, v_heads, morton_order, leaf_counts):
    heads_real, width, tokens = q_heads.shape
    heads = heads_real + heads_real % 2
    seq_count = lax.axis_size("seq")
    rows = heads * width
    flat = []
    for x in (q_heads, k_heads, v_heads):
        if heads != heads_real:
            x = jnp.concatenate([x, jnp.zeros_like(x[:1])], axis=0)
        flat.append(x.reshape(rows, tokens))
    leaves = tokens // LEAF
    depth_local = leaves.bit_length() - 1
    depth_all = (leaves * seq_count).bit_length() - 1
    levels = list(range(1, depth_all))
    far_levels = [l for l in levels if l >= depth_local]
    coarse = lambda l: min(LEAF, tokens >> l)
    vm = pltpu.VMEM
    scratch = [
        vm((3 * rows, tokens), BF),
        vm((2 * rows + PAD, tokens), BF),
        vm((tokens, 2 * rows), BF),
        vm((tokens + 2 * LEAF, rows), BF),
        vm((rows, tokens + 2 * LEAF), BF),
        vm((rows, tokens), F32),
        vm((2 * heads + (-2 * heads) % 8, tokens), F32),
    ]
    scratch += [vm((coarse(l), min(LEAF << l, tokens)), BF) for l in levels]
    scratch += [vm((heads, 2 * (width + PAD) + PAD, tokens >> l), BF) for l in levels]
    scratch += [vm((2 * rows, tokens >> l), BF) for l in far_levels]
    scratch += [vm((tokens >> l, 2 * rows), BF) for l in far_levels]
    scratch += [vm((2 * rows + PAD, tokens >> l), BF) for l in far_levels]
    scratch += [vm((LEAF, 2 * rows), BF) for l in far_levels]
    scratch += [
        vm((1 << (l - depth_local), 2 * rows + PAD, tokens >> l), BF) for l in far_levels
    ]
    sem = pltpu.SemaphoreType.DMA
    scratch += [sem((3,)), sem((4,)), sem((4,))]
    scratch += [sem((2 << (l - depth_local),)) for l in far_levels] * 2
    out = pl.pallas_call(
        functools.partial(kernel, (heads, width, tokens, seq_count)),
        out_shape=jax.ShapeDtypeStruct((rows, tokens), BF),
        in_specs=[pl.BlockSpec(memory_space=pl.ANY)] * 3
        + [
            pl.BlockSpec(memory_space=pltpu.VMEM),
            pl.BlockSpec(memory_space=pltpu.SMEM),
        ],
        out_specs=pl.BlockSpec(memory_space=pltpu.VMEM),
        scratch_shapes=scratch,
        compiler_params=pltpu.CompilerParams(
            collective_id=0, has_side_effects=True, vmem_limit_bytes=48 * 1024 * 1024
        ),
    )(*flat, morton_order, leaf_counts)
    return out.reshape(heads, width, tokens)[:heads_real]


def solution(mesh):
    placed = (
        P("head", None, ("grp", "seq")),
        P("head", None, ("grp", "seq")),
        P("head", None, ("grp", "seq")),
        P(("grp", "seq"), None),
        P("grp"),
    )
    return jax.shard_map(
        shards,
        mesh=mesh,
        in_specs=placed,
        out_specs=P("head", None, ("grp", "seq")),
        check_vma=False,
    )
```

profile of v0, /device:TPU:0, one launch (start us, length us, event | category | flops | bytes accessed | tf_op | source)
XLA Modules:
  0.0 36.8 jit_solution(1831834664561577317)
XLA Ops:
  0.0 0.0 copy-start.4
  0.0 0.7 %copy-done.4 = s32[32]{0:T(128)S(1)} copy-done((s32[32]{0:T(128)S(1)}, s32[32]{0:T(128)}, u32[]{:S(2)}) %copy-start.4) | copy-done | bytes 152
  0.7 0.0 copy-start
  0.7 1.0 %copy-done = bf16[2,64,2048]{2,1,0:T(8,128)(2,1)S(1)} copy-done((bf16[2,64,2048]{2,1,0:T(8,128)(2,1)S(1)}, bf16[2,64,2048]{2,1,0:T(8,128)(2,1)}, u32[]{:S(2)}) %copy-start) | copy-done | bytes 524312
  1.7 0.0 copy-start.1
  1.7 1.0 %copy-done.1 = bf16[2,64,2048]{2,1,0:T(8,128)(2,1)S(1)} copy-done((bf16[2,64,2048]{2,1,0:T(8,128)(2,1)S(1)}, bf16[2,64,2048]{2,1,0:T(8,128)(2,1)}, u32[]{:S(2)}) %copy-start.1) | copy-done | bytes 524312
  2.7 0.0 copy-start.2
  2.7 1.0 %copy-done.2 = bf16[2,64,2048]{2,1,0:T(8,128)(2,1)S(1)} copy-done((bf16[2,64,2048]{2,1,0:T(8,128)(2,1)S(1)}, bf16[2,64,2048]{2,1,0:T(8,128)(2,1)}, u32[]{:S(2)}) %copy-start.2) | copy-done | bytes 524312
  3.8 0.0 copy-start.3
  3.8 0.7 %copy-done.3 = s32[1,2048]{1,0:T(1,128)S(1)} copy-done((s32[1,2048]{1,0:T(1,128)S(1)}, s32[1,2048]{1,0:T(1,128)}, u32[]{:S(2)}) %copy-start.3) | copy-done | bytes 8216
  4.5 31.5 %shard_map.55 = bf16[128,2048]{1,0:T(8,128)(2,1)S(1)} custom-call(bf16[128,2048]{1,0:T(8,128)(2,1)S(1)} %bitcast.5, bf16[128,2048]{1,0:T(8,128)(2,1)S(1)} %bitcast.6, bf16[128,2048]{1,0:T(8,128)(2,1)S(1)} %bitcast.7, s32[1,2048]{1,0:T(1,128)S(1)} %copy-done.3, s32[32]{0:T(128)S(1)} %copy-done.4), custom_call_target="tpu_custom_call" | custom-call | tf_op jit(solution)/shard_map/pallas_call | solution.py:419
  36.0 0.8 %copy.7 = bf16[2,64,2048]{2,1,0:T(8,128)(2,1)} copy(bf16[2,64,2048]{2,1,0:T(8,128)(2,1)S(1)} %bitcast.4) | data formatting | bytes 1048576
Async XLA Ops:
  0.0 0.7 %copy-start.4 = (s32[32]{0:T(128)S(1)}, s32[32]{0:T(128)}, u32[]{:S(2)}) copy-start(s32[32]{0:T(128)} %refs_4_.1) | copy-start | bytes 388
  0.7 1.0 %copy-start = (bf16[2,64,2048]{2,1,0:T(8,128)(2,1)S(1)}, bf16[2,64,2048]{2,1,0:T(8,128)(2,1)}, u32[]{:S(2)}) copy-start(bf16[2,64,2048]{2,1,0:T(8,128)(2,1)} %param.5) | copy-start | bytes 1572868
  1.7 1.0 %copy-start.1 = (bf16[2,64,2048]{2,1,0:T(8,128)(2,1)S(1)}, bf16[2,64,2048]{2,1,0:T(8,128)(2,1)}, u32[]{:S(2)}) copy-start(bf16[2,64,2048]{2,1,0:T(8,128)(2,1)} %param.6) | copy-start | bytes 1572868
  2.7 1.0 %copy-start.2 = (bf16[2,64,2048]{2,1,0:T(8,128)(2,1)S(1)}, bf16[2,64,2048]{2,1,0:T(8,128)(2,1)}, u32[]{:S(2)}) copy-start(bf16[2,64,2048]{2,1,0:T(8,128)(2,1)} %param.7) | copy-start | bytes 1572868
  3.8 0.7 %copy-start.3 = (s32[1,2048]{1,0:T(1,128)S(1)}, s32[1,2048]{1,0:T(1,128)}, u32[]{:S(2)}) copy-start(s32[1,2048]{1,0:T(1,128)} %refs_3_.1) | copy-start | bytes 24580
where the time goes:
time: 37.1 us; the launch traced here: 36.8 us
  Pallas kernels  31.5 us (85%)
  local copies, waits for them, and re-layouts  5.27 us (14%)
    pallas_call x1, Pallas kernels, shards(): pl.pallas_call(functools.partial(kernel, (heads, width, tokens, seq_count...  31.5 us
    unnamed x11, local copies, waits for them, and re-layouts  5.27 us

commit v1 on v0

--- a/solution.py
+++ b/solution.py
@@ -13,6 +13,9 @@
 BF = jnp.bfloat16
 F32 = jnp.float32
 PAD = 16
+BOUND = 10.0
+STEPS = 32700.0
+VMEM_LIMIT = 63 * 1024 * 1024 + 512 * 1024
 
 
 def dot(a, b, dims=((1,), (0,))):
@@ -35,10 +38,12 @@
     scale = math.log2(math.e) / math.sqrt(width)
     refs = list(refs)
     take = lambda n: [refs.pop(0) for _ in range(n)]
-    q_hbm, k_hbm, v_hbm, order, counts, out = take(6)
+    q_hbm, k_hbm, v_hbm, order_hbm, counts_hbm, out = take(6)
+    order, counts = take(2)
     xin, xp, kva, ktx, vx, num, stat = take(7)
     us = dict(zip(levels, take(len(levels))))
-    fs = dict(zip(levels, take(len(levels))))
+    qb, kmb, vvb, biasb, fb = take(5)
+    fs = dict(zip(far_levels, take(len(far_levels))))
     qs = dict(zip(far_levels, take(len(far_levels))))
     kmp = dict(zip(far_levels, take(len(far_levels))))
     vvp = dict(zip(far_levels, take(len(far_levels))))
@@ -55,6 +60,8 @@
         pltpu.make_async_copy(src, xin.at[pl.ds(i * rows, rows)], in_sem.at[i])
         for i, src in enumerate((q_hbm, k_hbm, v_hbm))
     ]
+    loads.append(pltpu.make_async_copy(order_hbm, order, in_sem.at[3]))
+    loads.append(pltpu.make_async_copy(counts_hbm, counts, in_sem.at[4]))
     for load in loads:
         load.start()
     barrier = pltpu.get_barrier_semaphore()
@@ -112,10 +119,6 @@
         ktx[pl.ds(at + LEAF, LEAF), :] = key_t.astype(BF)
         vx[:, pl.ds(at + LEAF, LEAF)] = value.astype(BF)
 
-    permute(0)
-    permute(leaves - 1)
-    pl.semaphore_wait(barrier, seq_count - 1)
-
     def remote(src, dst, send, recv, target):
         return pltpu.make_async_remote_copy(
             src_ref=src,
@@ -146,42 +149,57 @@
             ),
         )
 
-    @pl.when(has_left)
-    def _():
-        for copy in halo(0):
-            copy.start()
-
-    @pl.when(has_right)
-    def _():
-        for copy in halo(1):
-            copy.start()
-
-    if leaves > 2:
-
-        @pl.loop(1, leaves - 1)
-        def _(n):
-            permute(n)
+    @pl.loop(0, leaves)
+    def _(i):
+        n = jnp.where(i == 0, 0, jnp.where(i == 1, leaves - 1, i - 1))
+        permute(n)
+
+        @pl.when(i == 1)
+        def _():
+            pl.semaphore_wait(barrier, seq_count - 1)
+
+        @pl.when(jnp.logical_and(i == 1, has_left))
+        def _():
+            for copy in halo(0):
+                copy.start()
+
+        @pl.when(jnp.logical_and(i == 1, has_right))
+        def _():
+            for copy in halo(1):
+                copy.start()
 
     def pool(level, off, span):
         u = us[level][...]
         kk = dot(u, kva[pl.ds(off, span), :])
         mass = kk[:, rows:]
-        km_hi, km_lo = split(kk[:, :rows] / jnp.maximum(mass, 1.0))
+        mean = kk[:, :rows] / jnp.maximum(mass, 1.0)
         xx = dot(xp[:, pl.ds(off, span)], u, ((1,), (1,)))
         q_hi, q_lo = split(xx[:rows] * (1.0 / 2**level))
-        v_hi, v_lo = split(xx[rows : 2 * rows])
-        km = jnp.concatenate([km_hi, km_lo], axis=1)
-        vv = jnp.concatenate([v_hi, v_lo, xx[2 * rows :].astype(BF)], axis=0)
-        return (q_hi, q_lo), km, vv, mass
+        return (q_hi, q_lo), mean, xx[rows : 2 * rows], xx[2 * rows :], mass
+
+    def pack(mean, sums, masses):
+        v_hi, v_lo = split(sums)
+        km = jnp.concatenate(split(mean), axis=1)
+        return km, jnp.concatenate([v_hi, v_lo, masses.astype(BF)], axis=0)
+
+    def fixed(x, bound):
+        return jnp.floor(x * (STEPS / bound) + 0.5).astype(jnp.int32).astype(jnp.int16)
+
+    def unfixed(x, bound):
+        return x.astype(jnp.int32).astype(F32) * (bound / STEPS)
+
+    def only(x, head):
+        blank = jnp.zeros((width, x.shape[1]), x.dtype)
+        return jnp.concatenate(
+            [x[h * width : (h + 1) * width] if h == head else blank for h in range(heads)],
+            axis=0,
+        )
 
     def far(query, km, vvs, bias, store):
         q_hi, q_lo = query
         count = q_hi.shape[1]
         for h in range(heads):
-            keep = lax.broadcasted_iota(jnp.int32, (rows, count), 0) // width == h
-            zero = jnp.zeros((rows, count), F32)
-            hi = jnp.where(keep, q_hi.astype(F32), zero).astype(BF)
-            lo = jnp.where(keep, q_lo.astype(F32), zero).astype(BF)
+            hi, lo = only(q_hi, h), only(q_lo, h)
             s = dot(km, jnp.concatenate([hi, hi], axis=0)) + dot(km[:, :rows], lo)
             if count <= 128:
                 s = s + bias[:, :count]
@@ -197,10 +215,9 @@
                 v_lo = vv[rows + h * width : rows + (h + 1) * width]
                 mass = vv[2 * rows :]
                 left = jnp.concatenate([v_hi, mass], axis=0)
-                acc = acc + dot(left, w_hi[step : step + keys])
-                acc = acc + dot(left, w_lo[step : step + keys])
-                low = dot(v_lo, w_hi[step : step + keys])
-                acc = acc + jnp.concatenate([low, jnp.zeros((PAD, count), F32)], axis=0)
+                both = dot(jnp.concatenate([left, v_lo], axis=0), w_hi[step : step + keys])
+                low = jnp.concatenate([both[width + PAD :], jnp.zeros((PAD, count), F32)], axis=0)
+                acc = acc + both[: width + PAD] + low + dot(left, w_lo[step : step + keys])
                 step += keys
             a_hi, a_lo = split(acc)
             tops = jnp.broadcast_to(best.astype(F32), (PAD, count)).astype(BF)
@@ -236,41 +253,56 @@
         return copies
 
     for level in reversed(far_levels):
-        (q_hi, q_lo), km, vv, _ = pool(level, 0, tokens)
+        (q_hi, q_lo), mean, sums, masses, _ = pool(level, 0, tokens)
         qs[level][0:rows, :] = q_hi
         qs[level][rows:, :] = q_lo
-        kmp[level][...] = km
-        vvp[level][...] = vv
+        kmp[level][...] = fixed(mean, BOUND)
+        vvp[level][0:rows, :] = fixed(sums, BOUND * 2**level)
+        vvp[level][rows:, :] = masses.astype(jnp.int32).astype(jnp.int16)
         for copy in far_copies(level):
             copy.start()
 
+    first = 0
     for level in levels:
         if level in far_levels:
             continue
         span = LEAF << level
-        for pair in range(tokens // span // 2):
-            sides = [pool(level, (2 * pair + i) * span, span) for i in range(2)]
-            for i in range(2):
-                query = sides[i][0]
-                _, km, vv, mass = sides[1 - i]
-                bias = jnp.where(mass > 0, 0.0, NEG)
-                first = (2 * pair + i) * LEAF
-
-                def store(h, value):
-                    fs[level][h, :, first : first + LEAF] = value
-
-                far(query, km, [vv], bias, store)
+        blocks = tokens // span
+        start = first
+
+        @pl.loop(0, blocks)
+        def _(i):
+            (q_hi, q_lo), mean, sums, masses, mass = pool(
+                level, pl.multiple_of(i * span, span), span
+            )
+            km, vv = pack(mean, sums, masses)
+            qb[start + i, 0:rows, :] = q_hi
+            qb[start + i, rows:, :] = q_lo
+            kmb[start + i] = km
+            vvb[start + i] = vv
+            biasb[start + i] = jnp.where(mass > 0, 0.0, NEG)
+
+        first += blocks
+
+    @pl.loop(0, first, unroll=2)
+    def _(i):
+        query = (qb[i, 0:rows, :], qb[i, rows:, :])
+        other = i + 1 - 2 * lax.rem(i, 2)
+
+        def store(h, value):
+            fb[i, h] = value
+
+        far(query, kmb[other], [vvb[other]], biasb[other], store)
 
     def near(n):
         at = n * LEAF
         if not isinstance(n, int):
             at = pl.multiple_of(at, LEAF)
         window = ktx[pl.ds(at, 3 * LEAF), :]
-        query = xp[0:rows, pl.ds(at, LEAF)].astype(F32)
+        query = xp[0:rows, pl.ds(at, LEAF)]
         spots = lax.broadcasted_iota(jnp.int32, (LEAF, LEAF), 0)
         for h in range(heads):
-            keep = lax.broadcasted_iota(jnp.int32, (rows, LEAF), 0) // width == h
-            s = dot(window, jnp.where(keep, query, 0.0).astype(BF))
+            s = dot(window, only(query, h))
             s = jnp.concatenate(
                 [
                     jnp.where(spots < count_of(n - 1 + i), s[i * LEAF : (i + 1) * LEAF], NEG)
@@ -288,7 +320,7 @@
 
     if leaves > 2:
 
-        @pl.loop(1, leaves - 1)
+        @pl.loop(1, leaves - 1, unroll=2)
         def _(n):
             near(n)
 
@@ -302,8 +334,9 @@
         for copy in halo(1):
             copy.wait_recv()
 
-    near(0)
-    near(leaves - 1)
+    @pl.loop(0, 2, unroll=2)
+    def _(i):
+        near(i * (leaves - 1))
 
     for level in far_levels:
         nb = 1 << (level - depth_local)
@@ -318,7 +351,13 @@
                 far_send[level].at[2 * i + 1], far_recv[level].at[2 * i + 1], seq,
             ).wait_recv()
         query = (qs[level][0:rows, :], qs[level][rows:, :])
-        vvs = [vvr[level][i] for i in range(nb)]
+        means = unfixed(kmr[level][...], BOUND)
+        vvs = []
+        for i in range(nb):
+            sums = unfixed(vvr[level][i, 0:rows], BOUND * 2**level)
+            masses = vvr[level][i, rows:].astype(jnp.int32).astype(F32)
+            km, vv = pack(means, sums, masses)
+            vvs.append(vv)
         ones = jnp.ones((PAD, 128), BF)
         mass = jnp.concatenate(
             [dot(vv[2 * rows :], ones, ((0,), (0,))) for vv in vvs], axis=0
@@ -328,7 +367,12 @@
         def store(h, value):
             fs[level][h] = value
 
-        far(query, kmr[level][...], vvs, bias, store)
+        far(query, km, vvs, bias, store)
+
+    base_of, first = {}, 0
+    for level in levels:
+        base_of[level] = first
+        first += tokens // (LEAF << level)
 
     def finish(n):
         at = pl.multiple_of(n * LEAF, LEAF)
@@ -344,7 +388,7 @@
                     u = us[level][:, pl.ds(at, LEAF)]
                 else:
                     g = 1 << level
-                    f = fs[level][h, :, pl.ds(pl.multiple_of((n >> level) * LEAF, LEAF), LEAF)]
+                    f = fb[base_of[level] + (n >> level), h]
                     u = us[level][:, pl.ds(pl.multiple_of((n & (g - 1)) * LEAF, LEAF), LEAF)]
                 up = dot(f, u)
                 top = up[2 * size : 2 * size + 1]
@@ -357,9 +401,9 @@
                 factor = jnp.exp2((level_best - best) * scale)
                 top = top + block[:width] * factor
                 bottom = bottom + block[width : width + 1] * factor
-            out[h * width : (h + 1) * width, pl.ds(at, LEAF)] = (top / bottom).astype(BF)
-
-    @pl.loop(0, leaves)
+            out[h * width : (h + 1) * width, pl.ds(at, LEAF)] = (top * (1.0 / bottom)).astype(BF)
+
+    @pl.loop(0, leaves, unroll=2)
     def _(n):
         finish(n)
 
@@ -396,6 +440,8 @@
     coarse = lambda l: min(LEAF, tokens >> l)
     vm = pltpu.VMEM
     scratch = [
+        vm(morton_order.shape, jnp.int32),
+        pltpu.SMEM(leaf_counts.shape, jnp.int32),
         vm((3 * rows, tokens), BF),
         vm((2 * rows + PAD, tokens), BF),
         vm((tokens, 2 * rows), BF),
@@ -405,29 +451,33 @@
         vm((2 * heads + (-2 * heads) % 8, tokens), F32),
     ]
     scratch += [vm((coarse(l), min(LEAF << l, tokens)), BF) for l in levels]
-    scratch += [vm((heads, 2 * (width + PAD) + PAD, tokens >> l), BF) for l in levels]
+    near_blocks = sum(tokens // (LEAF << l) for l in levels if l not in far_levels)
+    scratch += [
+        vm((near_blocks, 2 * rows, LEAF), BF),
+        vm((near_blocks, LEAF, 2 * rows), BF),
+        vm((near_blocks, 2 * rows + PAD, LEAF), BF),
+        vm((near_blocks, LEAF, rows), F32),
+        vm((near_blocks, heads, 2 * (width + PAD) + PAD, LEAF), BF),
+    ]
+    scratch += [vm((heads, 2 * (width + PAD) + PAD, tokens >> l), BF) for l in far_levels]
     scratch += [vm((2 * rows, tokens >> l), BF) for l in far_levels]
-    scratch += [vm((tokens >> l, 2 * rows), BF) for l in far_levels]
-    scratch += [vm((2 * rows + PAD, tokens >> l), BF) for l in far_levels]
-    scratch += [vm((LEAF, 2 * rows), BF) for l in far_levels]
+    scratch += [vm((tokens >> l, rows), jnp.int16) for l in far_levels]
+    scratch += [vm((rows + PAD, tokens >> l), jnp.int16) for l in far_levels]
+    scratch += [vm((LEAF, rows), jnp.int16) for l in far_levels]
     scratch += [
-        vm((1 << (l - depth_local), 2 * rows + PAD, tokens >> l), BF) for l in far_levels
+        vm((1 << (l - depth_local), rows + PAD, tokens >> l), jnp.int16) for l in far_levels
     ]
     sem = pltpu.SemaphoreType.DMA
-    scratch += [sem((3,)), sem((4,)), sem((4,))]
+    scratch += [sem((5,)), sem((4,)), sem((4,))]
     scratch += [sem((2 << (l - depth_local),)) for l in far_levels] * 2
     out = pl.pallas_call(
         functools.partial(kernel, (heads, width, tokens, seq_count)),
         out_shape=jax.ShapeDtypeStruct((rows, tokens), BF),
-        in_specs=[pl.BlockSpec(memory_space=pl.ANY)] * 3
-        + [
-            pl.BlockSpec(memory_space=pltpu.VMEM),
-            pl.BlockSpec(memory_space=pltpu.SMEM),
-        ],
+        in_specs=[pl.BlockSpec(memory_space=pltpu.HBM)] * 5,
         out_specs=pl.BlockSpec(memory_space=pltpu.VMEM),
         scratch_shapes=scratch,
         compiler_params=pltpu.CompilerParams(
-            collective_id=0, has_side_effects=True, vmem_limit_bytes=48 * 1024 * 1024
+            collective_id=0, has_side_effects=True, vmem_limit_bytes=VMEM_LIMIT
         ),
     )(*flat, morton_order, leaf_counts)
     return out.reshape(heads, width, tokens)[:heads_real]

time: 37.1 us -> 33.4 us (0.900)
  local copies, waits for them, and re-layouts: 5.27 us -> 1.88 us
    unnamed x11 -> x1, local copies, waits for them, and re-layouts: 5.27 us -> 1.88 us
where the time goes in v1:
time: 33.4 us; the launch traced here: 33.2 us
  Pallas kernels  31.3 us (94%)
  local copies, waits for them, and re-layouts  1.88 us (6%)
    pallas_call x1, Pallas kernels, shards(): pl.pallas_call(functools.partial(kernel, (heads, width, tokens, seq_count...  31.3 us
    unnamed x1, local copies, waits for them, and re-layouts  1.88 us

profile of v1, /device:TPU:0, one launch (start us, length us, event | category | flops | bytes accessed | tf_op | source)
XLA Modules:
  0.0 33.2 jit_solution(1598669959911226932)
XLA Ops:
  0.0 31.3 %shard_map.55 = bf16[128,2048]{1,0:T(8,128)(2,1)} custom-call(bf16[128,2048]{1,0:T(8,128)(2,1)} %bitcast.5, bf16[128,2048]{1,0:T(8,128)(2,1)} %bitcast.6, bf16[128,2048]{1,0:T(8,128)(2,1)} %bitcast.7, s32[1,2048]{1,0:T(1,128)} %refs_3_.1, s32[32]{0:T(128)} %refs_4_.1), custom_call_target="tpu_custom_call" | custom-call | tf_op jit(solution)/shard_map/pallas_call | solution.py:473
  31.3 1.9 %copy.7 = bf16[2,64,2048]{2,1,0:T(8,128)(2,1)} copy(bf16[2,64,2048]{2,1,0:T(8,128)(2,1)} %bitcast.4) | data formatting | bytes 1048576

commit v2 on v1

--- a/solution.py
+++ b/solution.py
@@ -103,8 +103,9 @@
         if not isinstance(n, int):
             at = pl.multiple_of(at, LEAF)
         picks = order[0:1, pl.ds(at, LEAF)]
-        spots = lax.broadcasted_iota(jnp.int32, (tokens, LEAF), 0)
-        hot = jnp.where(spots == picks, 1.0, 0.0).astype(BF)
+        spots = lax.broadcasted_iota(jnp.int16, (tokens, LEAF), 0)
+        wanted = jnp.broadcast_to(picks, (PAD, LEAF)).astype(jnp.int16)[0:1]
+        hot = jnp.where(spots == wanted, jnp.ones((), BF), jnp.zeros((), BF))
         moved = dot(xin[...], hot)
         count = count_of(n)
         query, key, value = moved[:rows], moved[rows : 2 * rows], moved[2 * rows :]

time: 33.4 us -> 33.4 us (level)
  no operation moved by 1% of the time
where the time goes in v2:
time: 33.4 us; the launch traced here: 33.3 us
  Pallas kernels  31.4 us (94%)
  local copies, waits for them, and re-layouts  1.88 us (6%)
    pallas_call x1, Pallas kernels, shards(): pl.pallas_call(functools.partial(kernel, (heads, width, tokens, seq_count...  31.4 us
    unnamed x1, local copies, waits for them, and re-layouts  1.88 us

profile of v2, /device:TPU:0, one launch (start us, length us, event | category | flops | bytes accessed | tf_op | source)
XLA Modules:
  0.0 33.3 jit_solution(3409011657948701242)
XLA Ops:
  0.0 31.4 %shard_map.55 = bf16[128,2048]{1,0:T(8,128)(2,1)} custom-call(bf16[128,2048]{1,0:T(8,128)(2,1)} %bitcast.5, bf16[128,2048]{1,0:T(8,128)(2,1)} %bitcast.6, bf16[128,2048]{1,0:T(8,128)(2,1)} %bitcast.7, s32[1,2048]{1,0:T(1,128)} %refs_3_.1, s32[32]{0:T(128)} %refs_4_.1), custom_call_target="tpu_custom_call" | custom-call | tf_op jit(solution)/shard_map/pallas_call | solution.py:474
  31.4 1.9 %copy.7 = bf16[2,64,2048]{2,1,0:T(8,128)(2,1)} copy(bf16[2,64,2048]{2,1,0:T(8,128)(2,1)} %bitcast.4) | data formatting | bytes 1048576
